TPU v7x, 256 devices: a whole 4x4x8 slice. The times are simulated.
256 devices in a mesh: dp: 8 (over z), expert: 32 (over y, x, core).
Axes of the slice: x: 4, y: 4, z: 8, core: 2. Of those that a mesh axis runs over, the one named last changes fastest.
Arguments:
- tokens: bfloat16 [32768, 4096], P(('dp', 'expert')), may hold values from -6 to 6
- cotangent: bfloat16 [32768, 4096], P(('dp', 'expert')), may hold values from -6 to 6
- expert_ids: int32 [32768, 2], P(('dp', 'expert')), may hold values from 0 to 15, all different within a row; in each aligned block of 128 rows (0 to 127, 128 to 255, ...) at most 18 rows name the same one
- probs: float32 [32768, 2], P(('dp', 'expert')), may hold values from 0.1 to 1
- w_gate: bfloat16 [32, 4096, 384], P('expert'), may hold values from -0.09375 to 0.09375
- w_up: bfloat16 [32, 4096, 384], P('expert'), may hold values from -0.09375 to 0.09375
- w_down: bfloat16 [32, 384, 4096], P('expert'), may hold values from -0.21875 to 0.21875
Outputs:
- grad_tokens: bfloat16 [32768, 4096], P(('dp', 'expert'))
- grad_gate: bfloat16 [32, 4096, 384], P('expert', 'dp')
- grad_up: bfloat16 [32, 4096, 384], P('expert', 'dp')
- grad_down: bfloat16 [32, 384, 4096], P('expert', None, 'dp')
Inputs may be any that keep to these rules, and one draw needn't show every extreme that they name: `expert_ids`: each row names 2 different experts; within each device block of 128 rows no expert is named by more than 18 rows, a bound that some block reaches.
All inputs are finite; a program needn't handle non-finite values.
Results may differ from a plain program's by a relative error of at most 0.019.
Values may be sent and summed in bfloat16 or wider, within the bound.
A program may use at most 128 MiB of HBM per device.

v0:
```python
import jax
import jax.numpy as jnp
from jax import lax
from jax.sharding import PartitionSpec as P


def slot_matrices(expert_ids, probs, experts_local, capacity):
    tok_count, top_count = expert_ids.shape
    flat_ids = expert_ids.reshape(-1)
    onehot = (flat_ids[:, None] == jnp.arange(experts_local, dtype=jnp.int32)[None, :]).astype(
        jnp.int32
    )
    ranks = jnp.cumsum(onehot, axis=0) - 1
    my_rank = jnp.sum(onehot * ranks, axis=1)
    slots = flat_ids * capacity + my_rank
    placed = (
        slots[:, None] == jnp.arange(experts_local * capacity, dtype=jnp.int32)[None, :]
    ).astype(jnp.float32)
    owners = jnp.arange(tok_count * top_count, dtype=jnp.int32) // top_count
    owner_onehot = (owners[:, None] == jnp.arange(tok_count, dtype=jnp.int32)[None, :]).astype(
        jnp.float32
    )
    picker = jnp.dot(placed.T, owner_onehot, preferred_element_type=jnp.float32).astype(
        jnp.bfloat16
    )
    slot_scale = jnp.dot(probs.reshape(-1), placed, precision=lax.Precision.HIGHEST)
    return (picker, slot_scale)


def shards(tokens, cotangent, expert_ids, probs, w_gate, w_up, w_down):
    n_devices = lax.axis_size("expert")
    experts_local = n_devices // 2
    tok_count, top_count = expert_ids.shape
    width = tokens.shape[1]
    capacity = (tok_count * top_count * 2 * 9 + 8 * n_devices - 1) // (8 * n_devices)
    picker, slot_scale = slot_matrices(expert_ids, probs, experts_local, capacity)
    x_slots = jnp.dot(picker, tokens, preferred_element_type=jnp.float32).astype(jnp.bfloat16)
    dy_slots = jnp.dot(picker, cotangent, preferred_element_type=jnp.float32)
    scaled_slots = (dy_slots * slot_scale[:, None]).astype(jnp.bfloat16)
    send_x = jnp.repeat(x_slots.reshape(experts_local, capacity, width), 2, axis=0)
    send_s = jnp.repeat(scaled_slots.reshape(experts_local, capacity, width), 2, axis=0)
    recv_x, recv_s = (
        lax.all_to_all(send_x, "expert", split_axis=0, concat_axis=0, tiled=True),
        lax.all_to_all(send_s, "expert", split_axis=0, concat_axis=0, tiled=True),
    )
    x_rows = recv_x.reshape(-1, width)
    scaled_rows = recv_s.reshape(-1, width)
    wg = w_gate[0]
    wu = w_up[0]
    wd = w_down[0]
    contract_last = (((1,), (1,)), ((), ()))
    contract_first = (((0,), (0,)), ((), ()))
    gate_pre = jnp.dot(x_rows, wg, preferred_element_type=jnp.float32)
    up_pre = jnp.dot(x_rows, wu, preferred_element_type=jnp.float32)
    sigmoid_gate = jax.nn.sigmoid(gate_pre)
    activated = gate_pre * sigmoid_gate
    hidden = (activated * up_pre).astype(jnp.bfloat16)
    grad_hidden = lax.dot_general(
        scaled_rows, wd, contract_last, preferred_element_type=jnp.float32
    )
    grad_gate_pre = (
        grad_hidden * up_pre * sigmoid_gate * (1.0 + gate_pre * (1.0 - sigmoid_gate))
    ).astype(jnp.bfloat16)
    grad_up_pre = (grad_hidden * activated).astype(jnp.bfloat16)
    row_grad = (
        lax.dot_general(grad_gate_pre, wg, contract_last, preferred_element_type=jnp.float32)
        + lax.dot_general(grad_up_pre, wu, contract_last, preferred_element_type=jnp.float32)
    ).astype(jnp.bfloat16)
    local_gate = lax.dot_general(
        x_rows, grad_gate_pre, contract_first, preferred_element_type=jnp.float32
    ).astype(jnp.bfloat16)
    local_up = lax.dot_general(
        x_rows, grad_up_pre, contract_first, preferred_element_type=jnp.float32
    ).astype(jnp.bfloat16)
    local_down = lax.dot_general(
        hidden, scaled_rows, contract_first, preferred_element_type=jnp.float32
    ).astype(jnp.bfloat16)
    returned = lax.all_to_all(
        row_grad.reshape(n_devices, capacity, width),
        "expert",
        split_axis=0,
        concat_axis=0,
        tiled=True,
    )
    both_halves = returned.reshape(experts_local, 2, capacity, width).astype(jnp.float32)
    pair_grad = (both_halves[:, 0] + both_halves[:, 1]).astype(jnp.bfloat16).reshape(-1, width)
    grad_tokens = lax.dot_general(
        picker, pair_grad, contract_first, preferred_element_type=jnp.float32
    ).astype(jnp.bfloat16)
    summed_gate, summed_up, summed_down = (
        lax.psum_scatter(local_gate[None], "dp", scatter_dimension=1, tiled=True).astype(
            jnp.float32
        ),
        lax.psum_scatter(local_up[None], "dp", scatter_dimension=1, tiled=True).astype(jnp.float32),
        lax.psum_scatter(local_down[None], "dp", scatter_dimension=2, tiled=True).astype(
            jnp.float32
        ),
    )
    return (
        grad_tokens,
        summed_gate.astype(jnp.bfloat16),
        summed_up.astype(jnp.bfloat16),
        summed_down.astype(jnp.bfloat16),
    )


def solution(mesh):
    in_specs = (
        P(("dp", "expert"), None),
        P(("dp", "expert"), None),
        P(("dp", "expert"), None),
        P(("dp", "expert"), None),
        P("expert", None, None),
        P("expert", None, None),
        P("expert", None, None),
    )
    out_specs = (
        P(("dp", "expert"), None),
        P("expert", "dp", None),
        P("expert", "dp", None),
        P("expert", None, "dp"),
    )
    return jax.shard_map(shards, mesh=mesh, in_specs=in_specs, out_specs=out_specs, check_vma=False)
```

profile of v0, /device:TPU:1, one launch (start us, length us, event | category | flops | bytes accessed | tf_op | source)
XLA Modules:
  0.0 360.0 jit_solution(8994257117485727814)
XLA Ops:
  7.2 0.9 copy.11
  8.4 0.6 reduce-window.6
  9.3 0.4 convolution_convert_fusion.5
  9.7 3.4 convolution_convert_fusion.3
  13.1 4.3 %reshape.90 = bf16[16,18,4096]{2,1,0:T(8,128)(2,1)} reshape(bf16[288,4096]{1,0:T(8,128)(2,1)} %convolution_convert_fusion.3) | data formatting | bytes 4718592 | tf_op jit(solution)/shard_map/reshape | solution.py:40
  17.4 5.3 %broadcast_in_dim.22 = bf16[16,2,18,4096]{3,2,1,0:T(8,128)(2,1)} broadcast(bf16[16,18,4096]{2,1,0:T(8,128)(2,1)} %reshape.90), dimensions={0,2,3} | broadcast | bytes 7077888 | tf_op jit(solution)/shard_map/broadcast_in_dim | solution.py:40
  22.8 8.8 %all-to-all-start.1 = ((bf16[32,18,4096]{2,1,0:T(8,128)(2,1)}), bf16[32,18,4096]{2,1,0:T(8,128)(2,1)}, u32[]{:S(2)}, u32[]{:S(2)}) async-start(bf16[32,18,4096]{2,1,0:T(8,128)(2,1)} %bitcast.69), calls=%async_computation.1 | async-start | bytes 12582912 | tf_op jit(solution)/shard_map/all_to_all | solution.py:43
  31.8 0.3 convolution_reduce_fusion
  32.1 3.4 fusion.2
  35.5 4.3 %reshape.87 = bf16[16,18,4096]{2,1,0:T(8,128)(2,1)} reshape(bf16[288,4096]{1,0:T(8,128)(2,1)} %fusion.2) | data formatting | bytes 4718592 | tf_op jit(solution)/shard_map/reshape | solution.py:41
  39.9 64.6 %all-to-all-done.1 = bf16[32,18,4096]{2,1,0:T(8,128)(2,1)} async-done(((bf16[32,18,4096]{2,1,0:T(8,128)(2,1)}), bf16[32,18,4096]{2,1,0:T(8,128)(2,1)}, u32[]{:S(2)}, u32[]{:S(2)}) %all-to-all-start.1) | async-done | bytes 4718624 | tf_op jit(solution)/shard_map/all_to_all | solution.py:43
  104.5 5.3 %broadcast_in_dim.10 = bf16[16,2,18,4096]{3,2,1,0:T(8,128)(2,1)} broadcast(bf16[16,18,4096]{2,1,0:T(8,128)(2,1)} %reshape.87), dimensions={0,2,3} | broadcast | bytes 7077888 | tf_op jit(solution)/shard_map/broadcast_in_dim | solution.py:41
  109.8 9.7 %all-to-all-start = ((bf16[32,18,4096]{2,1,0:T(8,128)(2,1)}), bf16[32,18,4096]{2,1,0:T(8,128)(2,1)}, u32[]{:S(2)}, u32[]{:S(2)}) async-start(bf16[32,18,4096]{2,1,0:T(8,128)(2,1)} %bitcast.70), calls=%async_computation | async-start | bytes 12582912 | tf_op jit(solution)/shard_map/all_to_all | solution.py:44
  119.6 7.7 %reshape.92 = bf16[576,4096]{1,0:T(8,128)(2,1)} reshape(bf16[32,18,4096]{2,1,0:T(8,128)(2,1)} %all-to-all-done.1) | data formatting | bytes 9437184 | tf_op jit(solution)/shard_map/reshape | solution.py:46
  127.3 6.0 %fusion.8 = f32[576,384]{1,0:T(8,128)} fusion(bf16[576,4096]{1,0:T(8,128)(2,1)} %reshape.92, bf16[1,4096,384]{2,1,0:T(8,128)(2,1)S(1)} %copy-done), kind=kOutput, calls=%fused_computation.17 | convolution fusion | flops 1811939328 | bytes 8749056 | tf_op jit(solution)/shard_map/dot_general | solution.py:53
  133.3 3.5 fusion.11
  136.8 55.8 %all-to-all-done = bf16[32,18,4096]{2,1,0:T(8,128)(2,1)} async-done(((bf16[32,18,4096]{2,1,0:T(8,128)(2,1)}), bf16[32,18,4096]{2,1,0:T(8,128)(2,1)}, u32[]{:S(2)}, u32[]{:S(2)}) %all-to-all-start) | async-done | bytes 4718624 | tf_op jit(solution)/shard_map/all_to_all | solution.py:44
  192.6 7.8 %reshape.89 = bf16[576,4096]{1,0:T(8,128)(2,1)} reshape(bf16[32,18,4096]{2,1,0:T(8,128)(2,1)} %all-to-all-done) | data formatting | bytes 9437184 | tf_op jit(solution)/shard_map/reshape | solution.py:47
  200.4 7.3 %fusion.5 = bf16[1,384,4096]{2,1,0:T(8,128)(2,1)} fusion(bf16[576,4096]{1,0:T(8,128)(2,1)} %reshape.89, f32[576,384]{1,0:T(8,128)} %fusion.11, f32[576,384]{1,0:T(8,128)} %fusion.8), kind=kOutput, calls=%fused_computation.13 | convolution fusion | flops 1814839296 | bytes 9633792 | tf_op jit(solution)/shard_map/dot_general | solution.py:75
  207.9 7.3 %multiply_convert_fusion.1 = (bf16[576,384]{1,0:T(8,128)(2,1)}, bf16[576,384]{1,0:T(8,128)(2,1)S(1)}) fusion(f32[576,384]{1,0:T(8,128)} %fusion.8, f32[576,384]{1,0:T(8,128)} %fusion.11, bf16[576,4096]{1,0:T(8,128)(2,1)} %reshape.89, bf16[1,384,4096]{2,1,0:T(8,128)(2,1)} %param.13), kind=kOutput, calls=%fused_computation.27 | convolution fusion | flops 1814814720 | bytes 10518528 | tf_op jit(solution)/shard_map/dot_general | solution.py:58
  215.2 0.8 copy-done.3
  216.0 7.3 %fusion.3 = bf16[1,4096,384]{2,1,0:T(8,128)(2,1)} fusion(bf16[576,4096]{1,0:T(8,128)(2,1)} %reshape.92, bf16[576,384]{1,0:T(8,128)(2,1)S(1)} %get-tuple-element.5), kind=kOutput, calls=%fused_computation.11 | convolution fusion | flops 1813512192 | bytes 8306688 | tf_op jit(solution)/shard_map/dot_general | solution.py:69
  223.3 7.4 %fusion.4 = bf16[1,4096,384]{2,1,0:T(8,128)(2,1)} fusion(bf16[576,4096]{1,0:T(8,128)(2,1)} %reshape.92, bf16[576,384]{1,0:T(8,128)(2,1)} %get-tuple-element.4), kind=kOutput, calls=%fused_computation.12 | convolution fusion | flops 1813512192 | bytes 8306688 | tf_op jit(solution)/shard_map/dot_general | solution.py:72
  230.7 6.1 %fusion.6 = f32[576,4096]{1,0:T(8,128)} fusion(bf16[576,384]{1,0:T(8,128)(2,1)} %copy-done.3, bf16[1,4096,384]{2,1,0:T(8,128)(2,1)S(1)} %copy-done), kind=kOutput, calls=%fused_computation.15 | convolution fusion | flops 1811939328 | bytes 13025280 | tf_op jit(solution)/shard_map/dot_general | solution.py:66
  236.8 9.8 %add_convert_fusion = bf16[576,4096]{1,0:T(8,128)(2,1)} fusion(f32[576,4096]{1,0:T(8,128)} %fusion.6, bf16[576,384]{1,0:T(8,128)(2,1)} %get-tuple-element.4, bf16[1,4096,384]{2,1,0:T(8,128)(2,1)} %param.12), kind=kOutput, calls=%fused_computation | convolution fusion | flops 1816657920 | bytes 17743872 | tf_op jit(solution)/shard_map/dot_general | solution.py:67
  246.6 7.6 %reshape.93 = bf16[32,18,4096]{2,1,0:T(8,128)(2,1)} reshape(bf16[576,4096]{1,0:T(8,128)(2,1)} %add_convert_fusion) | data formatting | bytes 9437184 | tf_op jit(solution)/shard_map/reshape | solution.py:79
  254.2 83.8 %all_to_all.15 = bf16[32,18,4096]{2,1,0:T(8,128)(2,1)} all-to-all(bf16[32,18,4096]{2,1,0:T(8,128)(2,1)} %reshape.93), channel_id=1, replica_groups=mesh['dp'=8,'expert'=32] {'expert'}, dimensions={0} | all-to-all | bytes 9437184 | tf_op jit(solution)/shard_map/all_to_all | solution.py:78
  338.0 4.6 %convert.1 = f32[16,2,18,4096]{3,2,1,0:T(8,128)S(1)} convert(bf16[16,2,18,4096]{3,2,1,0:T(8,128)(2,1)} %bitcast.71) | non-fusion elementwise | flops 2359296 | bytes 14155776 | tf_op jit(solution)/shard_map/convert_element_type | solution.py:85
  342.6 2.5 fusion.1
  345.1 4.4 %convert_element_type.69 = bf16[288,4096]{1,0:T(8,128)(2,1)} reshape(bf16[16,1,18,4096]{3,2,0,1:T(8,128)(2,1)} %fusion.1) | data formatting | bytes 4718592 | tf_op jit(solution)/shard_map/convert_element_type | solution.py:86
  349.4 3.4 convolution_convert_fusion.4
  352.9 0.6 reduce-scatter.6.cloned.1.call-done
  (27 shorter events, 1.2 us)
Async XLA Ops:
  7.2 120.2 %copy-start = (bf16[1,4096,384]{2,1,0:T(8,128)(2,1)S(1)}, bf16[1,4096,384]{2,1,0:T(8,128)(2,1)}, u32[]{:S(2)}) copy-start(bf16[1,4096,384]{2,1,0:T(8,128)(2,1)} %param.11) | copy-start | bytes 9437188
  22.8 8.8 %copy-start.4 = (f32[128,2]{0,1:T(2,128)S(1)}, f32[128,2]{0,1:T(2,128)}, u32[]{:S(2)}) copy-start(f32[128,2]{0,1:T(2,128)} %param.10) | copy-start | bytes 3076
  22.8 81.7 %all-to-all-start.1 = ((bf16[32,18,4096]{2,1,0:T(8,128)(2,1)}), bf16[32,18,4096]{2,1,0:T(8,128)(2,1)}, u32[]{:S(2)}, u32[]{:S(2)}) async-start(bf16[32,18,4096]{2,1,0:T(8,128)(2,1)} %bitcast.69), calls=%async_computation.1 | async-start | bytes 12582912 | tf_op jit(solution)/shard_map/all_to_all | solution.py:43
  109.8 82.8 %all-to-all-start = ((bf16[32,18,4096]{2,1,0:T(8,128)(2,1)}), bf16[32,18,4096]{2,1,0:T(8,128)(2,1)}, u32[]{:S(2)}, u32[]{:S(2)}) async-start(bf16[32,18,4096]{2,1,0:T(8,128)(2,1)} %bitcast.70), calls=%async_computation | async-start | bytes 12582912 | tf_op jit(solution)/shard_map/all_to_all | solution.py:44
  119.6 233.3 %reduce-scatter.8.cloned.1.call-start = ((), (), s32[]{:S(2)}) async-start(), calls=%async_computation.8 | async-start | bytes 3538944 | tf_op jit(solution)/shard_map/reduce_scatter | solution.py:95
  127.3 6.0 %copy-start.1 = (bf16[576,4096]{1,0:T(8,128)(2,1)S(1)}, bf16[576,4096]{1,0:T(8,128)(2,1)}, u32[]{:S(2)}) copy-start(bf16[576,4096]{1,0:T(8,128)(2,1)} %reshape.92) | copy-start | bytes 14155780
  127.3 6.0 %copy-start.2 = (bf16[1,4096,384]{2,1,0:T(8,128)(2,1)S(1)}, bf16[1,4096,384]{2,1,0:T(8,128)(2,1)}, u32[]{:S(2)}) copy-start(bf16[1,4096,384]{2,1,0:T(8,128)(2,1)} %param.12) | copy-start | bytes 9437188
  207.7 145.2 %reduce-scatter.4.cloned.1.call-start = ((), (), s32[]{:S(2)}) async-start(), calls=%async_computation.6 | async-start | bytes 3538944 | tf_op jit(solution)/shard_map/reduce_scatter | solution.py:91
  215.2 0.8 copy-start.3
  223.2 130.2 %reduce-scatter.6.cloned.1.call-start = ((), (), s32[]{:S(2)}) async-start(), calls=%async_computation.7 | async-start | bytes 3538944 | tf_op jit(solution)/shard_map/reduce_scatter | solution.py:94
Sparse Core Ops, SparseCore 0:
  207.8 47.2 reduce-scatter.7
  258.2 45.9 reduce-scatter.3
  307.4 46.0 reduce-scatter.5
where the time goes:
time: 363 us; the launch traced here: 360 us
  waiting for transfers between devices  121 us (33%)
  blocking collectives  83.8 us (23%)
  matrix products  65.5 us (18%)
  local copies, waits for them, and re-layouts  49.3 us (14%)
  starting transfers between devices  18.8 us (5%)
  between operations  13.8 us (4%)
  other arithmetic  7.79 us (2%)
    all_to_all x1, blocking collectives, shards(): lax.all_to_all(row_grad.reshape(n_devices, capacity, width), 'expert', sp...  83.8 us
    all_to_all x1, waiting for transfers between devices, shards(): lax.all_to_all(send_x, 'expert', split_axis=0, concat_axis=0, tiled=True)  64.6 us
    all_to_all x1, waiting for transfers between devices, shards(): lax.all_to_all(send_s, 'expert', split_axis=0, concat_axis=0, tiled=True)  55.8 us
    dot_general x1, matrix products, shards(): lax.dot_general(grad_up_pre, wu, contract_last, preferred_element_type=jn...  9.82 us
    all_to_all x1, starting transfers between devices, shards(): lax.all_to_all(send_s, 'expert', split_axis=0, concat_axis=0, tiled=True)  9.72 us
    all_to_all x1, starting transfers between devices, shards(): lax.all_to_all(send_x, 'expert', split_axis=0, concat_axis=0, tiled=True)  8.77 us
    reshape x1, local copies, waits for them, and re-layouts, shards(): scaled_rows = recv_s.reshape(-1, width)  7.81 us
    reshape x1, local copies, waits for them, and re-layouts, shards(): x_rows = recv_x.reshape(-1, width)  7.73 us
  transfers between devices with their start and end apart: 5, of which 3 were waited for; matrix products, arithmetic and copies ran while one was open for 24% of the time, Pallas kernels for 0%

commit v1 on v0

v1 whole, which is shorter than its diff:
```python
import jax
import jax.numpy as jnp
from jax import lax
from jax.experimental import pallas as pl
from jax.experimental.pallas import tpu as pltpu
from jax.sharding import PartitionSpec as P

D = 4096
F = 384
TOK = 128
N_DP = 8
CHIPS = 16
J = 8
DS = D // J
MAIN = 16
HALF = CHIPS * MAIN
ROWS = 2 * HALF + 64
UNIT = 96
MESH = pl.DeviceIdType.MESH
F32 = jnp.float32
BF16 = jnp.bfloat16
OTHERS = (
    (0, 1), (1, 0), (0, 3), (3, 0), (1, 1), (3, 3), (1, 3), (3, 1),
    (0, 2), (2, 0), (2, 1), (1, 2), (2, 3), (3, 2), (2, 2),
)
X_AT, XE_AT, S_AT, SE_AT, R_AT, RE_AT = 0, 4, 5, 13, 14, 18
RG_AT, RGE_AT = 14, 22


def mm(a, b):
    return jnp.dot(a, b, preferred_element_type=F32)


def mm_nt(a, b):
    return lax.dot_general(a, b, (((1,), (1,)), ((), ())), preferred_element_type=F32)


def iota(shape, dim):
    return lax.broadcasted_iota(jnp.int32, shape, dim)


def eye(n):
    return (iota((n, n), 0) == iota((n, n), 1)).astype(BF16)


def kernel(
    ids, probs, tok, cot, wg, wu, wd,
    gt, grads,
    tokb, cotb, w_gu, w_d, xs, xse, ss, sse, X, XE, S, SE,
    pick, pick_e, pick_t, pick_et, scales, pre, gh, ggu, at,
    RG, RGE, RV, RVE, PS, PSE, RT, RTE, ring, gts, gds,
    loc, snd, rcv, sib_s, sib_r, ring_s, ring_r,
):
    z = lax.axis_index("dp")
    e = lax.axis_index("expert")
    k = lax.rem(e, 2)
    c = e // 2
    cy = c // 4
    cx = lax.rem(c, 4)
    sibling = (z, c * 2 + (1 - k))
    z_next = (lax.rem(z + 1, N_DP), e)
    z_prev = (lax.rem(z + N_DP - 1, N_DP), e)
    chip_of = [lax.rem(cy + dy, 4) * 4 + lax.rem(cx + dx, 4) for dy, dx in OTHERS]

    for j in range(J):
        cols = pl.ds(j * DS, DS)
        pltpu.make_async_copy(tok.at[:, cols], tokb.at[j], loc.at[0]).start()
    for j in range(J):
        cols = pl.ds(j * DS, DS)
        pltpu.make_async_copy(cot.at[:, cols], cotb.at[j], loc.at[1]).start()
    barrier = pltpu.get_barrier_semaphore()
    for chip in chip_of:
        pl.semaphore_signal(barrier, inc=1, device_id=(z, chip * 2 + k), device_id_type=MESH)
    for dev in (sibling, z_next, z_prev):
        pl.semaphore_signal(barrier, inc=1, device_id=dev, device_id_type=MESH)
    for j in range(J):
        rows = pl.ds(j * DS, DS)
        pltpu.make_async_copy(wg.at[rows, :], w_gu.at[j, :, pl.ds(0, F)], loc.at[2]).start()
        pltpu.make_async_copy(wu.at[rows, :], w_gu.at[j, :, pl.ds(F, F)], loc.at[2]).start()
    for j in range(J):
        pltpu.make_async_copy(wd.at[:, pl.ds(j * DS, DS)], w_d.at[j], loc.at[3]).start()

    def wait_bytes(ref, sem):
        pltpu.make_async_copy(ref, ref, sem).wait()

    id0, id1 = ids[0:1, :], ids[1:2, :]
    p0, p1 = probs[0:1, :], probs[1:2, :]
    row = iota((HALF, TOK), 0)
    expert, slot = row // MAIN, lax.rem(row, MAIN)
    named0, named1 = id0 == expert, id1 == expert
    named = named0 | named1
    before = (iota((TOK, TOK), 0) < iota((TOK, TOK), 1)).astype(BF16)
    rank = mm(named.astype(F32).astype(BF16), before).astype(jnp.int32)
    main = named & (rank == slot)
    extra = named & (rank == MAIN + lax.rem(slot, 2))
    pick[...] = main.astype(F32).astype(BF16)
    pick_e[...] = extra.astype(F32).astype(BF16)

    def scale_of(picked):
        each = jnp.where(picked & named0, p0, 0.0) + jnp.where(picked & named1, p1, 0.0)
        return jnp.broadcast_to(jnp.sum(each, axis=1, keepdims=True), (HALF, TOK))

    scales[0] = scale_of(main)
    scales[1] = scale_of(extra)
    part = lax.rem(iota((HALF, TOK), 0), MAIN) // 2

    def extras_of(source):
        def add(j, total):
            chosen = jnp.where(part == j, pick_e[...].astype(F32), 0.0).astype(BF16)
            return total + mm(chosen, source[j])
        return lax.fori_loop(0, J, add, jnp.zeros((HALF, DS), F32))

    def blk(i):
        return pl.ds(pl.multiple_of(i * MAIN, MAIN), MAIN)

    def home(i):
        return pl.ds(pl.multiple_of(k * HALF + i * MAIN, MAIN), MAIN)

    mine = pl.ds(pl.multiple_of(k * HALF, HALF), HALF)
    theirs = pl.ds(pl.multiple_of((1 - k) * HALF, HALF), HALF)

    def send_all(src_of, dst, at_sem):
        for chip in chip_of:
            pltpu.make_async_remote_copy(
                src_ref=src_of(chip), dst_ref=dst,
                send_sem=snd.at[at_sem], recv_sem=rcv.at[at_sem],
                device_id=(z, chip * 2 + k), device_id_type=MESH,
            ).start()
        pltpu.make_async_copy(src_of(c), dst, rcv.at[at_sem]).start()

    def to_sibling(src, dst, at_sem):
        return pltpu.make_async_remote_copy(
            src_ref=src, dst_ref=dst, send_sem=sib_s.at[at_sem], recv_sem=sib_r.at[at_sem],
            device_id=sibling, device_id_type=MESH,
        )

    wait_bytes(tokb, loc.at[0])
    xse[...] = extras_of(tokb).astype(BF16)
    pl.semaphore_wait(barrier, len(OTHERS) + 3)
    send_all(lambda i: xse.at[blk(i), :], XE.at[home(c), :], XE_AT)

    @pl.loop(0, 4)
    def _(q):
        for n in range(2):
            xs[2 * q + n] = mm(pick[...], tokb[2 * q + n]).astype(BF16)
        two = pl.ds(2 * q, 2)
        send_all(lambda i: xs.at[two, blk(i), :], X.at[two, home(c), :], X_AT + q)

    wait_bytes(cotb, loc.at[1])
    sse[...] = (extras_of(cotb) * scales[1][:, 0:1]).astype(BF16)
    pick_t[...] = mm_nt(eye(TOK), pick[...]).astype(BF16)
    pick_et[...] = mm_nt(eye(TOK), pick_e[...]).astype(BF16)
    for u in range(12):
        ring[u, 0] = jnp.zeros((UNIT, DS), BF16)
    pre[...] = jnp.zeros_like(pre)
    gh[...] = jnp.zeros_like(gh)

    def order(i):
        pair = i // 2
        first = lax.rem(z + 15 - pair, N_DP)
        second = lax.rem(z + 1 + pair + 4 * (pair // 3), N_DP)
        odd = lax.rem(i, 2)
        return first * (1 - odd) + second * odd

    def send_cot(i):
        o = order(i)
        ss[o] = (mm(pick[...], cotb[o]) * scales[0][:, 0:1]).astype(BF16)
        send_all(lambda n: ss.at[o, blk(n), :], S.at[o, home(c), :], S_AT + i)

    def unpack(j):
        r, col = iota((64, 2 * HALF), 0), iota((64, 2 * HALF), 1)
        return (col == (r // 2) * MAIN + 2 * j + lax.rem(r, 2)).astype(F32).astype(BF16)

    def unpack_t(j):
        r, col = iota((2 * HALF, 64), 1), iota((2 * HALF, 64), 0)
        return (col == (r // 2) * MAIN + 2 * j + lax.rem(r, 2)).astype(F32).astype(BF16)

    tail = pl.ds(2 * HALF, 64)

    wait_bytes(XE.at[pl.ds(0, HALF), :], rcv.at[XE_AT])
    fwd_xe = to_sibling(XE.at[mine, :], XE.at[mine, :], XE_AT)
    fwd_xe.start()
    fwd_xe.wait_recv()

    @pl.loop(0, J)
    def _(j):
        X[j, tail, :] = mm(unpack(j), XE[...]).astype(BF16)

    send_all(lambda i: sse.at[blk(i), :], SE.at[home(c), :], SE_AT)
    wait_bytes(w_gu, loc.at[2])

    @pl.loop(0, 4)
    def _(q):
        two = pl.ds(2 * q, 2)
        wait_bytes(X.at[two, pl.ds(0, HALF), :], rcv.at[X_AT + q])
        fwd = to_sibling(X.at[two, mine, :], X.at[two, mine, :], X_AT + q)
        fwd.start()
        send_cot(2 * q)
        send_cot(2 * q + 1)
        fwd.wait_recv()
        pre[...] += mm(X[2 * q], w_gu[2 * q]) + mm(X[2 * q + 1], w_gu[2 * q + 1])

    def store_t(first, value):
        at[pl.ds(first, F), :] = mm_nt(eye(F), value).astype(BF16)

    gate, up = pre[:, 0:F], pre[:, F:2 * F]
    store_t(2 * F, (gate * jax.nn.sigmoid(gate) * up).astype(BF16))

    def ring_step(t, forward, group, source):
        u0, units, first = group
        d = lax.rem(z + 15 - t, N_DP) if forward else lax.rem(z + 1 + t, N_DP)
        part_sum = mm(at[pl.ds(first, units * UNIT), :], source[d])
        for n in range(units):
            u = u0 + n
            slot_ref = ring.at[u, t]

            @pl.when(t > 0)
            def _():
                wait_bytes(slot_ref, ring_r.at[u, t])

            total = (part_sum[n * UNIT:(n + 1) * UNIT] + slot_ref[...].astype(F32)).astype(BF16)

            @pl.when(t < N_DP - 1)
            def _():
                slot_ref[...] = total
                pltpu.make_async_remote_copy(
                    src_ref=slot_ref, dst_ref=ring.at[u, t + 1],
                    send_sem=ring_s.at[u, t], recv_sem=ring_r.at[u, t + 1],
                    device_id=z_next if forward else z_prev, device_id_type=MESH,
                ).start()

            @pl.when(t == N_DP - 1)
            def _():
                gds[pl.ds(first + n * UNIT, UNIT), :] = total

    def ring_down(t):
        ring_step(t, True, (0, 2, 2 * F), S)
        ring_step(t, False, (2, 2, 2 * F + 192), S)

    def ring_gate_up(t):
        ring_step(t, True, (4, 4, 0), X)
        ring_step(t, False, (8, 4, F), X)

    wait_bytes(SE.at[pl.ds(0, HALF), :], rcv.at[SE_AT])
    fwd_se = to_sibling(SE.at[mine, :], SE.at[mine, :], SE_AT)
    fwd_se.start()
    fwd_se.wait_recv()
    wait_bytes(w_d, loc.at[3])

    @pl.loop(0, 4)
    def _(pair):
        for n in range(2):
            i = 2 * pair + n
            o = order(i)
            wait_bytes(S.at[o, pl.ds(0, HALF), :], rcv.at[S_AT + i])
            to_sibling(S.at[o, mine, :], S.at[o, mine, :], S_AT + i).start()
        for n in range(2):
            i = 2 * pair + n
            o = order(i)
            S[o, tail, :] = mm(unpack(o), SE[...]).astype(BF16)
            to_sibling(S.at[o, mine, :], S.at[o, mine, :], S_AT + i).wait_recv()
        ring_down(pair)
        for n in range(2):
            o = order(2 * pair + n)
            gh[...] += mm_nt(S[o], w_d[o])

    gate, up, grad = pre[:, 0:F], pre[:, F:2 * F], gh[...]
    sig = jax.nn.sigmoid(gate)
    ggate = (grad * up * sig * (1.0 + gate * (1.0 - sig))).astype(BF16)
    gup = (grad * gate * sig).astype(BF16)
    ggu[:, 0:F] = ggate
    ggu[:, F:2 * F] = gup
    store_t(0, ggate)
    store_t(F, gup)

    def row_grad(j):
        RG[j] = mm_nt(ggu[...], w_gu[j]).astype(BF16)
        to_sibling(RG.at[j, theirs, :], RV.at[j], RG_AT + j).start()

    def pair_grad(q):
        for n in range(2):
            j = 2 * q + n
            to_sibling(RG.at[j, theirs, :], RV.at[j], RG_AT + j).wait_recv()
            PS[j] = (RG[j, mine, :].astype(F32) + RV[j].astype(F32)).astype(BF16)
        two = pl.ds(2 * q, 2)
        send_all(lambda i: PS.at[two, blk(i), :], RT.at[two, blk(c), :], R_AT + q)

    def row_grad_extras():
        def add(j, total):
            return total + mm(unpack_t(j), RG[j, tail, :])
        RGE[...] = lax.fori_loop(0, J, add, jnp.zeros((2 * HALF, DS), F32)).astype(BF16)
        to_sibling(RGE.at[theirs, :], RVE, RGE_AT).start()

    def pair_grad_extras():
        to_sibling(RGE.at[theirs, :], RVE, RGE_AT).wait_recv()
        PSE[...] = (RGE[mine, :].astype(F32) + RVE[...].astype(F32)).astype(BF16)
        send_all(lambda i: PSE.at[blk(i), :], RTE.at[blk(c), :], RE_AT)

    part_col = lax.rem(iota((TOK, HALF), 1), MAIN) // 2

    def token_grad(q):
        two = pl.ds(2 * q, 2)
        wait_bytes(RT.at[two], rcv.at[R_AT + q])
        for n in range(2):
            j = 2 * q + n
            chosen = jnp.where(part_col == j, pick_et[...].astype(F32), 0.0).astype(BF16)
            gts[j] = (mm(pick_t[...], RT[j]) + mm(chosen, RTE[...])).astype(BF16)
            pltpu.make_async_copy(gts.at[j], gt.at[j], loc.at[4]).start()

    @pl.loop(0, N_DP)
    def _(t):
        ring_gate_up(t)

        @pl.when(t < 4)
        def _():
            ring_down(t + 4)
            row_grad(2 * t)
            row_grad(2 * t + 1)

        @pl.when((t > 0) & (t < 5))
        def _():
            pair_grad(t - 1)

        @pl.when(t == 4)
        def _():
            row_grad_extras()

        @pl.when(t == 5)
        def _():
            pair_grad_extras()

        @pl.when(t == 6)
        def _():
            wait_bytes(RTE, rcv.at[RE_AT])

            @pl.loop(0, 4)
            def _(q):
                token_grad(q)

    out = pltpu.make_async_copy(gds, grads, loc.at[5])
    out.start()

    def sent(ref, sem):
        wait_bytes(ref, sem)

    less = HALF - MAIN
    for q in range(4):
        two = pl.ds(2 * q, 2)
        sent(xs.at[two, pl.ds(0, less), :], snd.at[X_AT + q])
        sent(PS.at[two, pl.ds(0, less), :], snd.at[R_AT + q])
        sent(X.at[two, pl.ds(0, HALF), :], sib_s.at[X_AT + q])
    for i in range(J):
        sent(ss.at[i, pl.ds(0, less), :], snd.at[S_AT + i])
        sent(ss.at[i], sib_s.at[S_AT + i])
        sent(RV.at[i], sib_s.at[RG_AT + i])
    for at_sem in (XE_AT, SE_AT, RE_AT):
        sent(xse.at[pl.ds(0, less), :], snd.at[at_sem])
    for at_sem in (XE_AT, SE_AT, RGE_AT):
        sent(xse, sib_s.at[at_sem])

    @pl.loop(0, N_DP - 1)
    def _(t):
        for u in range(12):
            sent(ring.at[u, t], ring_s.at[u, t])

    wait_bytes(gts, loc.at[4])
    out.wait()


def shards(tokens, cotangent, expert_ids, probs, w_gate, w_up, w_down):
    any_ = pl.BlockSpec(memory_space=pl.ANY)
    vmem = pl.BlockSpec(memory_space=pltpu.VMEM)
    dma = pltpu.SemaphoreType.DMA
    v = pltpu.VMEM
    gt, grads = pl.pallas_call(
        kernel,
        out_shape=(
            jax.ShapeDtypeStruct((J, TOK, DS), BF16),
            jax.ShapeDtypeStruct((3 * F, DS), BF16),
        ),
        in_specs=[vmem, vmem] + [any_] * 5,
        out_specs=(any_, any_),
        scratch_shapes=[
            v((J, TOK, DS), BF16), v((J, TOK, DS), BF16),
            v((J, DS, 2 * F), BF16), v((J, F, DS), BF16),
            v((J, HALF, DS), BF16), v((HALF, DS), BF16),
            v((J, HALF, DS), BF16), v((HALF, DS), BF16),
            v((J, ROWS, DS), BF16), v((2 * HALF, DS), BF16),
            v((J, ROWS, DS), BF16), v((2 * HALF, DS), BF16),
            v((HALF, TOK), BF16), v((HALF, TOK), BF16),
            v((TOK, HALF), BF16), v((TOK, HALF), BF16),
            v((2, HALF, TOK), F32),
            v((ROWS, 2 * F), F32), v((ROWS, F), F32),
            v((ROWS, 2 * F), BF16), v((3 * F, ROWS), BF16),
            v((J, ROWS, DS), BF16), v((2 * HALF, DS), BF16),
            v((J, HALF, DS), BF16), v((HALF, DS), BF16),
            v((J, HALF, DS), BF16), v((HALF, DS), BF16),
            v((J, HALF, DS), BF16), v((HALF, DS), BF16),
            v((12, N_DP, UNIT, DS), BF16),
            v((J, TOK, DS), BF16), v((3 * F, DS), BF16),
            dma((6,)), dma((19,)), dma((19,)), dma((23,)), dma((23,)),
            dma((12, N_DP)), dma((12, N_DP)),
        ],
        compiler_params=pltpu.CompilerParams(
            collective_id=0, has_side_effects=True, vmem_limit_bytes=60 * 2**20
        ),
        cost_estimate=pl.CostEstimate(
            flops=15_000_000_000, bytes_accessed=14_000_000, transcendentals=500_000
        ),
    )(expert_ids.T, probs.T, tokens, cotangent, w_gate[0], w_up[0], w_down[0])
    return (
        gt.transpose(1, 0, 2).reshape(TOK, D),
        grads[0:F].T[None],
        grads[F:2 * F].T[None],
        grads[2 * F:][None],
    )


def solution(mesh):
    in_specs = (
        P(("dp", "expert"), None),
        P(("dp", "expert"), None),
        P(("dp", "expert"), None),
        P(("dp", "expert"), None),
        P("expert", None, None),
        P("expert", None, None),
        P("expert", None, None),
    )
    out_specs = (
        P(("dp", "expert"), None),
        P("expert", "dp", None),
        P("expert", "dp", None),
        P("expert", None, "dp"),
    )
    return jax.shard_map(shards, mesh=mesh, in_specs=in_specs, out_specs=out_specs, check_vma=False)
```

time: 363 us -> 157 us (0.43)
  Pallas kernels: 0 us -> 151 us
  waiting for transfers between devices: 121 us -> 0 us
  blocking collectives: 83.8 us -> 0 us
  matrix products: 65.5 us -> 0 us
  local copies, waits for them, and re-layouts: 49.3 us -> 5.68 us
  starting transfers between devices: 18.8 us -> 0 us
  between operations: 13.8 us -> 0.66 us
  other arithmetic: 7.79 us -> 0 us
    pallas_call x0 -> x1, Pallas kernels: none -> 151 us  [shards(): pl.pallas_call(kernel, out_shape=(jax.ShapeDtypeStruct((J, TOK, DS), BF16...]
    all_to_all x2 -> x0, waiting for transfers between devices: 120 us -> none  [the longest x1 64.6 us: shards(): lax.all_to_all(send_x, 'expert', split_axis=0, concat_axis=0, tiled=True)]
    all_to_all x1 -> x0, blocking collectives: 83.8 us -> none  [shards(): lax.all_to_all(row_grad.reshape(n_devices, capacity, width), 'expert', sp...]
    dot_general x13 -> x0, matrix products: 65.5 us -> none  [the longest x1 9.82 us: shards(): lax.dot_general(grad_up_pre, wu, contract_last, preferred_element_type=jn...]
    reshape x7 -> x0, local copies, waits for them, and re-layouts: 32.1 us -> none  [the longest x1 7.81 us: shards(): scaled_rows = recv_s.reshape(-1, width)]
    all_to_all x2 -> x0, starting transfers between devices: 18.5 us -> none  [the longest x1 9.72 us: shards(): lax.all_to_all(send_s, 'expert', split_axis=0, concat_axis=0, tiled=True)]
    broadcast_in_dim x2 -> x1, local copies, waits for them, and re-layouts: 10.7 us -> 0.82 us  [shards(): grads[2 * F:][None]]
    convert_element_type x3 -> x0, other arithmetic: 7.07 us -> none  [the longest x1 4.6 us: shards(): returned.reshape(experts_local, 2, capacity, width).astype(jnp.float32)]
  transfers between devices with their start and end apart: 5 -> 0, of which waited for: 3 -> 0; matrix products, arithmetic and copies ran while one was open for 24% -> 0% of each run, Pallas kernels for 0% -> 0%
where the time goes in v1:
time: 157 us
  Pallas kernels  151 us (96%)
  local copies, waits for them, and re-layouts  5.68 us (4%)
    pallas_call x1, Pallas kernels, shards(): pl.pallas_call(kernel, out_shape=(jax.ShapeDtypeStruct((J, TOK, DS), BF16...  151 us
    unnamed x5, local copies, waits for them, and re-layouts  3.15 us

profile of v1, /device:TPU:1, one launch (start us, length us, event | category | flops | bytes accessed | tf_op | source)
XLA Modules:
  0.0 157.2 jit_solution(8252071925762233692)
XLA Ops:
  0.6 150.8 %shard_map.102 = (bf16[8,128,512]{2,1,0:T(8,128)(2,1)}, bf16[1152,512]{1,0:T(8,128)(2,1)}) custom-call(s32[2,128]{1,0:T(2,128)} %bitcast.22, f32[2,128]{1,0:T(2,128)} %bitcast.23, bf16[128,4096]{1,0:T(8,128)(2,1)} %tok.1, bf16[128,4096]{1,0:T(8,128)(2,1)} %cot.1, bf16[4096,384]{1,0:T(8,128)(2,1)} %bitcast.19, bf16[4096,384]{1,0:T(8,128)(2,1)} %bitcast.20, ...), custom_call_target="tpu_custom_call" | custom-call | flops 15000000512 | bytes 14000000 | tf_op jit(solution)/shard_map/pallas_call | solution.py:375
  151.5 0.0 copy-start
  151.5 1.7 %copy.13 = bf16[128,8,512]{0,2,1:T(8,128)(2,1)S(1)} copy(bf16[128,8,512]{2,0,1:T(8,128)(2,1)} %bitcast.18) | data formatting | bytes 2097152 | tf_op jit(solution)/shard_map/transpose | solution.py:412
  153.2 1.3 copy.14
  154.5 0.0 copy-done
  154.5 0.8 slice_bitcast_fusion
  155.3 0.9 copy.16
  156.3 0.9 copy.15
Async XLA Ops:
  151.5 3.0 %copy-start = (bf16[1152,512]{1,0:T(8,128)(2,1)S(1)}, bf16[1152,512]{1,0:T(8,128)(2,1)}, u32[]{:S(2)}) copy-start(bf16[1152,512]{1,0:T(8,128)(2,1)} %get-tuple-element.7) | copy-start | bytes 3538948

commit v2 on v1

--- a/solution.py
+++ b/solution.py
@@ -23,8 +23,9 @@
     (0, 1), (1, 0), (0, 3), (3, 0), (1, 1), (3, 3), (1, 3), (3, 1),
     (0, 2), (2, 0), (2, 1), (1, 2), (2, 3), (3, 2), (2, 2),
 )
-X_AT, XE_AT, S_AT, SE_AT, R_AT, RE_AT = 0, 4, 5, 13, 14, 18
-RG_AT, RGE_AT = 14, 22
+X_AT, XE_AT, S_AT, SE_AT, R_AT, RE_AT = 0, 8, 9, 17, 18, 22
+RG_AT, RGE_AT = 18, 26
+LAG = 2
 
 
 def mm(a, b):
@@ -45,10 +46,10 @@
 
 def kernel(
     ids, probs, tok, cot, wg, wu, wd,
-    gt, grads,
+    gt, gg, gu, gd,
     tokb, cotb, w_gu, w_d, xs, xse, ss, sse, X, XE, S, SE,
     pick, pick_e, pick_t, pick_et, scales, pre, gh, ggu, at,
-    RG, RGE, RV, RVE, PS, PSE, RT, RTE, ring, gts, gds,
+    RG, RGE, RV, RVE, PS, PSE, RT, RTE, ring, begin, psum, gds, outs,
     loc, snd, rcv, sib_s, sib_r, ring_s, ring_r,
 ):
     z = lax.axis_index("dp")
@@ -62,23 +63,14 @@
     z_prev = (lax.rem(z + N_DP - 1, N_DP), e)
     chip_of = [lax.rem(cy + dy, 4) * 4 + lax.rem(cx + dx, 4) for dy, dx in OTHERS]
 
-    for j in range(J):
-        cols = pl.ds(j * DS, DS)
-        pltpu.make_async_copy(tok.at[:, cols], tokb.at[j], loc.at[0]).start()
-    for j in range(J):
-        cols = pl.ds(j * DS, DS)
-        pltpu.make_async_copy(cot.at[:, cols], cotb.at[j], loc.at[1]).start()
     barrier = pltpu.get_barrier_semaphore()
+    for dev in (z_next, z_prev):
+        pl.semaphore_signal(barrier, inc=1, device_id=dev, device_id_type=MESH)
     for chip in chip_of:
         pl.semaphore_signal(barrier, inc=1, device_id=(z, chip * 2 + k), device_id_type=MESH)
-    for dev in (sibling, z_next, z_prev):
-        pl.semaphore_signal(barrier, inc=1, device_id=dev, device_id_type=MESH)
+    pl.semaphore_signal(barrier, inc=1, device_id=sibling, device_id_type=MESH)
     for j in range(J):
-        rows = pl.ds(j * DS, DS)
-        pltpu.make_async_copy(wg.at[rows, :], w_gu.at[j, :, pl.ds(0, F)], loc.at[2]).start()
-        pltpu.make_async_copy(wu.at[rows, :], w_gu.at[j, :, pl.ds(F, F)], loc.at[2]).start()
-    for j in range(J):
-        pltpu.make_async_copy(wd.at[:, pl.ds(j * DS, DS)], w_d.at[j], loc.at[3]).start()
+        pltpu.make_async_copy(tok.at[:, pl.ds(j * DS, DS)], tokb.at[j], loc.at[0]).start()
 
     def wait_bytes(ref, sem):
         pltpu.make_async_copy(ref, ref, sem).wait()
@@ -135,32 +127,43 @@
         )
 
     wait_bytes(tokb, loc.at[0])
+
+    def send_tok(j):
+        send_all(lambda i: xs.at[j, blk(i), :], X.at[j, home(c), :], X_AT + j)
+
+    xs[0] = mm(pick[...], tokb[0]).astype(BF16)
+    pl.semaphore_wait(barrier, len(OTHERS) + 3)
+    send_tok(0)
     xse[...] = extras_of(tokb).astype(BF16)
-    pl.semaphore_wait(barrier, len(OTHERS) + 3)
     send_all(lambda i: xse.at[blk(i), :], XE.at[home(c), :], XE_AT)
 
-    @pl.loop(0, 4)
-    def _(q):
-        for n in range(2):
-            xs[2 * q + n] = mm(pick[...], tokb[2 * q + n]).astype(BF16)
-        two = pl.ds(2 * q, 2)
-        send_all(lambda i: xs.at[two, blk(i), :], X.at[two, home(c), :], X_AT + q)
+    @pl.loop(1, J)
+    def _(j):
+        xs[j] = mm(pick[...], tokb[j]).astype(BF16)
+        send_tok(j)
+
+    for j in range(J):
+        pltpu.make_async_copy(cot.at[:, pl.ds(j * DS, DS)], cotb.at[j], loc.at[1]).start()
+    for j in range(J):
+        rows = pl.ds(j * DS, DS)
+        pltpu.make_async_copy(wg.at[rows, :], w_gu.at[j, :, pl.ds(0, F)], loc.at[2]).start()
+        pltpu.make_async_copy(wu.at[rows, :], w_gu.at[j, :, pl.ds(F, F)], loc.at[2]).start()
+    for j in range(J):
+        pltpu.make_async_copy(wd.at[:, pl.ds(j * DS, DS)], w_d.at[j], loc.at[3]).start()
 
     wait_bytes(cotb, loc.at[1])
     sse[...] = (extras_of(cotb) * scales[1][:, 0:1]).astype(BF16)
     pick_t[...] = mm_nt(eye(TOK), pick[...]).astype(BF16)
     pick_et[...] = mm_nt(eye(TOK), pick_e[...]).astype(BF16)
-    for u in range(12):
-        ring[u, 0] = jnp.zeros((UNIT, DS), BF16)
     pre[...] = jnp.zeros_like(pre)
     gh[...] = jnp.zeros_like(gh)
 
+    def place(t, up):
+        return lax.rem(z + 12 - t, N_DP) if up else lax.rem(z + 4 + t, N_DP)
+
     def order(i):
-        pair = i // 2
-        first = lax.rem(z + 15 - pair, N_DP)
-        second = lax.rem(z + 1 + pair + 4 * (pair // 3), N_DP)
         odd = lax.rem(i, 2)
-        return first * (1 - odd) + second * odd
+        return place((i + 1) // 2, True) * odd + place(i // 2, False) * (1 - odd)
 
     def send_cot(i):
         o = order(i)
@@ -189,16 +192,22 @@
     send_all(lambda i: sse.at[blk(i), :], SE.at[home(c), :], SE_AT)
     wait_bytes(w_gu, loc.at[2])
 
-    @pl.loop(0, 4)
-    def _(q):
-        two = pl.ds(2 * q, 2)
-        wait_bytes(X.at[two, pl.ds(0, HALF), :], rcv.at[X_AT + q])
-        fwd = to_sibling(X.at[two, mine, :], X.at[two, mine, :], X_AT + q)
+    @pl.loop(0, J)
+    def _(j):
+        wait_bytes(X.at[j, pl.ds(0, HALF), :], rcv.at[X_AT + j])
+        fwd = to_sibling(X.at[j, mine, :], X.at[j, mine, :], X_AT + j)
         fwd.start()
-        send_cot(2 * q)
-        send_cot(2 * q + 1)
+
+        @pl.when(j >= LAG)
+        def _():
+            send_cot(j - LAG)
+
         fwd.wait_recv()
-        pre[...] += mm(X[2 * q], w_gu[2 * q]) + mm(X[2 * q + 1], w_gu[2 * q + 1])
+        pre[...] += mm(X[j], w_gu[j])
+
+    @pl.loop(J - LAG, J)
+    def _(i):
+        send_cot(i)
 
     def store_t(first, value):
         at[pl.ds(first, F), :] = mm_nt(eye(F), value).astype(BF16)
@@ -206,40 +215,67 @@
     gate, up = pre[:, 0:F], pre[:, F:2 * F]
     store_t(2 * F, (gate * jax.nn.sigmoid(gate) * up).astype(BF16))
 
-    def ring_step(t, forward, group, source):
-        u0, units, first = group
-        d = lax.rem(z + 15 - t, N_DP) if forward else lax.rem(z + 1 + t, N_DP)
-        part_sum = mm(at[pl.ds(first, units * UNIT), :], source[d])
-        for n in range(units):
-            u = u0 + n
-            slot_ref = ring.at[u, t]
-
-            @pl.when(t > 0)
-            def _():
-                wait_bytes(slot_ref, ring_r.at[u, t])
-
-            total = (part_sum[n * UNIT:(n + 1) * UNIT] + slot_ref[...].astype(F32)).astype(BF16)
-
-            @pl.when(t < N_DP - 1)
-            def _():
-                slot_ref[...] = total
-                pltpu.make_async_remote_copy(
-                    src_ref=slot_ref, dst_ref=ring.at[u, t + 1],
-                    send_sem=ring_s.at[u, t], recv_sem=ring_r.at[u, t + 1],
-                    device_id=z_next if forward else z_prev, device_id_type=MESH,
-                ).start()
-
-            @pl.when(t == N_DP - 1)
-            def _():
-                gds[pl.ds(first + n * UNIT, UNIT), :] = total
-
-    def ring_down(t):
-        ring_step(t, True, (0, 2, 2 * F), S)
-        ring_step(t, False, (2, 2, 2 * F + 192), S)
-
-    def ring_gate_up(t):
-        ring_step(t, True, (4, 4, 0), X)
-        ring_step(t, False, (8, 4, F), X)
+    def pass_on(v, t, src, up):
+        pltpu.make_async_remote_copy(
+            src_ref=src, dst_ref=ring.at[v, t],
+            send_sem=ring_s.at[v, t], recv_sem=ring_r.at[v, t],
+            device_id=z_next if up else z_prev, device_id_type=MESH,
+        ).start()
+
+    down, gate_up = (0, 4, 2 * F), (4, 8, 0)
+
+    def begin_chains(group, source):
+        u0, n, first = group
+        terms = mm(at[pl.ds(first, n * UNIT), :], source[place(0, False)])
+        for m in range(n):
+            begin[u0 + m] = terms[m * UNIT:(m + 1) * UNIT].astype(BF16)
+
+        @pl.loop(0, n // 2)
+        def _(m):
+            pass_on(u0 + m, 0, begin.at[u0 + m], False)
+            pass_on(12 + u0 + n // 2 + m, 0, begin.at[u0 + n // 2 + m], True)
+
+    def terms_of(group, t, up, source):
+        u0, n, first = group
+        terms = mm(at[pl.ds(first, n * UNIT), :], source[place(t, up)])
+        for m in range(n):
+            psum[up * 8 + m] = terms[m * UNIT:(m + 1) * UNIT]
+
+    def hop(group, m, t, up, joins):
+        v = up * 12 + group[0] + m
+        slot_ref = ring.at[v, t - 1]
+        if joins:
+            wait_bytes(slot_ref, ring_r.at[v, t - 1])
+            slot_ref[...] = (psum[up * 8 + m] + slot_ref[...].astype(F32)).astype(BF16)
+        else:
+            slot_ref[...] = psum[up * 8 + m].astype(BF16)
+        pass_on(v, t, slot_ref, up)
+
+    def hops(group, t, half, ups):
+        n = group[1]
+
+        @pl.loop(0, n // 2)
+        def _(m):
+            joins = t > 1 or half == 1
+            for up in ups:
+                upper = (half == 0) != bool(up)
+                hop(group, m + (n // 2 if upper else 0), t, up, joins)
+
+    def end_chains(group, source):
+        u0, n, first = group
+        terms_of(group, 4, 0, source)
+
+        def end(m):
+            for up in range(2):
+                wait_bytes(ring.at[up * 12 + u0 + m, 3], ring_r.at[up * 12 + u0 + m, 3])
+            came = ring[u0 + m, 3].astype(F32) + ring[12 + u0 + m, 3].astype(F32)
+            rows = pl.ds(pl.multiple_of(first + m * UNIT, UNIT), UNIT)
+            gds[rows, :] = (psum[m] + came).astype(BF16)
+
+        @pl.loop(0, n // 2)
+        def _(m):
+            end(m)
+            end(n // 2 + m)
 
     wait_bytes(SE.at[pl.ds(0, HALF), :], rcv.at[SE_AT])
     fwd_se = to_sibling(SE.at[mine, :], SE.at[mine, :], SE_AT)
@@ -247,22 +283,38 @@
     fwd_se.wait_recv()
     wait_bytes(w_d, loc.at[3])
 
-    @pl.loop(0, 4)
-    def _(pair):
-        for n in range(2):
-            i = 2 * pair + n
-            o = order(i)
-            wait_bytes(S.at[o, pl.ds(0, HALF), :], rcv.at[S_AT + i])
-            to_sibling(S.at[o, mine, :], S.at[o, mine, :], S_AT + i).start()
-        for n in range(2):
-            i = 2 * pair + n
-            o = order(i)
-            S[o, tail, :] = mm(unpack(o), SE[...]).astype(BF16)
-            to_sibling(S.at[o, mine, :], S.at[o, mine, :], S_AT + i).wait_recv()
-        ring_down(pair)
-        for n in range(2):
-            o = order(2 * pair + n)
-            gh[...] += mm_nt(S[o], w_d[o])
+    def forward(i):
+        o = order(i)
+        wait_bytes(S.at[o, pl.ds(0, HALF), :], rcv.at[S_AT + i])
+        to_sibling(S.at[o, mine, :], S.at[o, mine, :], S_AT + i).start()
+        S[o, tail, :] = mm(unpack(o), SE[...]).astype(BF16)
+
+    def here(i):
+        o = order(i)
+        to_sibling(S.at[o, mine, :], S.at[o, mine, :], S_AT + i).wait_recv()
+
+    def grad_hidden(i):
+        o = order(i)
+        gh[...] += mm_nt(S[o], w_d[o])
+
+    def down_step(t, up):
+        terms_of(down, t, up, S)
+        hops(down, t, 0, (up,))
+        hops(down, t, 1, (up,))
+
+    forward(0)
+    here(0)
+    begin_chains(down, S)
+    for i in range(1, 7):
+        forward(i)
+        grad_hidden(i - 1)
+        here(i)
+        if i == 6:
+            forward(7)
+        down_step((i + 1) // 2, i % 2)
+    grad_hidden(6)
+    here(7)
+    grad_hidden(7)
 
     gate, up, grad = pre[:, 0:F], pre[:, F:2 * F], gh[...]
     sig = jax.nn.sigmoid(gate)
@@ -304,41 +356,40 @@
         for n in range(2):
             j = 2 * q + n
             chosen = jnp.where(part_col == j, pick_et[...].astype(F32), 0.0).astype(BF16)
-            gts[j] = (mm(pick_t[...], RT[j]) + mm(chosen, RTE[...])).astype(BF16)
-            pltpu.make_async_copy(gts.at[j], gt.at[j], loc.at[4]).start()
-
-    @pl.loop(0, N_DP)
-    def _(t):
-        ring_gate_up(t)
-
-        @pl.when(t < 4)
-        def _():
-            ring_down(t + 4)
-            row_grad(2 * t)
-            row_grad(2 * t + 1)
-
-        @pl.when((t > 0) & (t < 5))
-        def _():
-            pair_grad(t - 1)
-
-        @pl.when(t == 4)
-        def _():
+            tokb[j] = (mm(pick_t[...], RT[j]) + mm(chosen, RTE[...])).astype(BF16)
+            cols = pl.ds(pl.multiple_of(j * DS, DS), DS)
+            pltpu.make_async_copy(tokb.at[j], gt.at[:, cols], loc.at[4]).start()
+
+    def several(first, last, what):
+        @pl.loop(first, last)
+        def _(n):
+            what(n)
+
+    begin_chains(gate_up, X)
+    several(0, 4, row_grad)
+    for t in range(1, 4):
+        terms_of(gate_up, t, 1, X)
+        terms_of(gate_up, t, 0, X)
+        hops(gate_up, t, 0, (1, 0))
+        if t == 1:
+            several(4, 8, row_grad)
+            pair_grad(0)
+            pair_grad(1)
+        if t == 2:
+            pair_grad_extras()
+        hops(gate_up, t, 1, (1, 0))
+        if t == 1:
+            several(2, 4, pair_grad)
             row_grad_extras()
-
-        @pl.when(t == 5)
-        def _():
-            pair_grad_extras()
-
-        @pl.when(t == 6)
-        def _():
-            wait_bytes(RTE, rcv.at[RE_AT])
-
-            @pl.loop(0, 4)
-            def _(q):
-                token_grad(q)
-
-    out = pltpu.make_async_copy(gds, grads, loc.at[5])
-    out.start()
+    end_chains(down, S)
+    pltpu.make_async_copy(gds.at[pl.ds(2 * F, F), :], gd, loc.at[5]).start()
+    wait_bytes(RTE, rcv.at[RE_AT])
+    several(0, 4, token_grad)
+    end_chains(gate_up, X)
+    out_d = pltpu.make_async_copy(gds.at[pl.ds(2 * F, F), :], gd, loc.at[5])
+    for n, dst in enumerate((gg, gu)):
+        outs[n] = mm_nt(eye(DS), gds[n * F:(n + 1) * F, :]).astype(BF16)
+        pltpu.make_async_copy(outs.at[n], dst, loc.at[6 + n]).start()
 
     def sent(ref, sem):
         wait_bytes(ref, sem)
@@ -346,11 +397,11 @@
     less = HALF - MAIN
     for q in range(4):
         two = pl.ds(2 * q, 2)
-        sent(xs.at[two, pl.ds(0, less), :], snd.at[X_AT + q])
         sent(PS.at[two, pl.ds(0, less), :], snd.at[R_AT + q])
-        sent(X.at[two, pl.ds(0, HALF), :], sib_s.at[X_AT + q])
     for i in range(J):
+        sent(xs.at[i, pl.ds(0, less), :], snd.at[X_AT + i])
         sent(ss.at[i, pl.ds(0, less), :], snd.at[S_AT + i])
+        sent(xs.at[i], sib_s.at[X_AT + i])
         sent(ss.at[i], sib_s.at[S_AT + i])
         sent(RV.at[i], sib_s.at[RG_AT + i])
     for at_sem in (XE_AT, SE_AT, RE_AT):
@@ -358,13 +409,35 @@
     for at_sem in (XE_AT, SE_AT, RGE_AT):
         sent(xse, sib_s.at[at_sem])
 
-    @pl.loop(0, N_DP - 1)
-    def _(t):
-        for u in range(12):
-            sent(ring.at[u, t], ring_s.at[u, t])
-
-    wait_bytes(gts, loc.at[4])
-    out.wait()
+    @pl.loop(0, 24)
+    def _(v):
+        for t in range(1, 4):
+            sent(ring.at[v, t], ring_s.at[v, t])
+
+    for u0, n, _ in (down, gate_up):
+        for m in range(n // 2):
+            sent(begin.at[0], ring_s.at[u0 + m, 0])
+            sent(begin.at[0], ring_s.at[12 + u0 + n // 2 + m, 0])
+
+    wait_bytes(tokb, loc.at[4])
+    out_d.wait()
+    for n, dst in enumerate((gg, gu)):
+        pltpu.make_async_copy(outs.at[n], dst, loc.at[6 + n]).wait()
+
+
+def write_out(gt, gg, gu, gd, gt_out, gg_out, gu_out, gd_out, gt_v, gg_v, gu_v, gd_v, sem):
+    whole = ((gg, gg_v, gg_out), (gu, gu_v, gu_out), (gd, gd_v, gd_out))
+    parts = [tuple(ref.at[pl.ds(32 * n, 32), :] for ref in (gt, gt_v, gt_out)) for n in range(4)]
+    parts += whole
+    reads = [pltpu.make_async_copy(src, mid, sem.at[0, n]) for n, (src, mid, _) in enumerate(parts)]
+    writes = [pltpu.make_async_copy(mid, dst, sem.at[1, n]) for n, (_, mid, dst) in enumerate(parts)]
+    for read in reads:
+        read.start()
+    for read, write in zip(reads, writes):
+        read.wait()
+        write.start()
+    for write in writes:
+        write.wait()
 
 
 def shards(tokens, cotangent, expert_ids, probs, w_gate, w_up, w_down):
@@ -372,14 +445,16 @@
     vmem = pl.BlockSpec(memory_space=pltpu.VMEM)
     dma = pltpu.SemaphoreType.DMA
     v = pltpu.VMEM
-    gt, grads = pl.pallas_call(
+    gt, gg, gu, gd = pl.pallas_call(
         kernel,
         out_shape=(
-            jax.ShapeDtypeStruct((J, TOK, DS), BF16),
-            jax.ShapeDtypeStruct((3 * F, DS), BF16),
+            jax.ShapeDtypeStruct((TOK, D), BF16),
+            jax.ShapeDtypeStruct((DS, F), BF16),
+            jax.ShapeDtypeStruct((DS, F), BF16),
+            jax.ShapeDtypeStruct((F, DS), BF16),
         ),
         in_specs=[vmem, vmem] + [any_] * 5,
-        out_specs=(any_, any_),
+        out_specs=(any_,) * 4,
         scratch_shapes=[
             v((J, TOK, DS), BF16), v((J, TOK, DS), BF16),
             v((J, DS, 2 * F), BF16), v((J, F, DS), BF16),
@@ -396,10 +471,10 @@
             v((J, HALF, DS), BF16), v((HALF, DS), BF16),
             v((J, HALF, DS), BF16), v((HALF, DS), BF16),
             v((J, HALF, DS), BF16), v((HALF, DS), BF16),
-            v((12, N_DP, UNIT, DS), BF16),
-            v((J, TOK, DS), BF16), v((3 * F, DS), BF16),
-            dma((6,)), dma((19,)), dma((19,)), dma((23,)), dma((23,)),
-            dma((12, N_DP)), dma((12, N_DP)),
+            v((24, 4, UNIT, DS), BF16), v((12, UNIT, DS), BF16), v((16, UNIT, DS), F32),
+            v((3 * F, DS), BF16), v((2, DS, F), BF16),
+            dma((8,)), dma((23,)), dma((23,)), dma((27,)), dma((27,)),
+            dma((24, 4)), dma((24, 4)),
         ],
         compiler_params=pltpu.CompilerParams(
             collective_id=0, has_side_effects=True, vmem_limit_bytes=60 * 2**20
@@ -408,12 +483,15 @@
             flops=15_000_000_000, bytes_accessed=14_000_000, transcendentals=500_000
         ),
     )(expert_ids.T, probs.T, tokens, cotangent, w_gate[0], w_up[0], w_down[0])
-    return (
-        gt.transpose(1, 0, 2).reshape(TOK, D),
-        grads[0:F].T[None],
-        grads[F:2 * F].T[None],
-        grads[2 * F:][None],
-    )
+    found = (gt, gg, gu, gd)
+    gt, gg, gu, gd = pl.pallas_call(
+        write_out,
+        out_shape=tuple(jax.ShapeDtypeStruct(a.shape, a.dtype) for a in found),
+        in_specs=[any_] * 4,
+        out_specs=(any_,) * 4,
+        scratch_shapes=[v(a.shape, a.dtype) for a in found] + [dma((2, 7))],
+    )(*found)
+    return gt, gg[None], gu[None], gd[None]
 
 
 def solution(mesh):

time: 157 us -> 147 us (0.936)
  local copies, waits for them, and re-layouts: 5.68 us -> 0 us
  Pallas kernels: 151 us -> 146 us
    pallas_call x1 -> x2, Pallas kernels: 151 us -> 146 us  [the longest x1 144 us: shards(): pl.pallas_call(kernel, out_shape=(jax.ShapeDtypeStruct((TOK, D), BF16), j...]
    unnamed x5 -> x0, local copies, waits for them, and re-layouts: 3.15 us -> none
    transpose x1 -> x0, local copies, waits for them, and re-layouts: 1.71 us -> none  [shards(): gt.transpose(1, 0, 2).reshape(TOK, D)]
where the time goes in v2:
time: 147 us
  Pallas kernels  146 us (99%)
    pallas_call x1, Pallas kernels, shards(): pl.pallas_call(kernel, out_shape=(jax.ShapeDtypeStruct((TOK, D), BF16), j...  144 us

profile of v2, /device:TPU:1, one launch (start us, length us, event | category | flops | bytes accessed | tf_op | source)
XLA Modules:
  0.0 147.0 jit_solution(7010548139734737076)
XLA Ops:
  0.6 143.9 %shard_map.102 = (bf16[128,4096]{1,0:T(8,128)(2,1)}, bf16[512,384]{1,0:T(8,128)(2,1)}, bf16[512,384]{1,0:T(8,128)(2,1)}, bf16[384,512]{1,0:T(8,128)(2,1)}) custom-call(s32[2,128]{1,0:T(2,128)} %bitcast.14, f32[2,128]{1,0:T(2,128)} %bitcast.15, bf16[128,4096]{1,0:T(8,128)(2,1)} %tok.1, bf16[128,4096]{1,0:T(8,128)(2,1)} %cot.1, bf16[4096,384]{1,0:T(8,128)(2,1)} %bitcast.8, ...), custom_call_target="tpu_custom_call" | custom-call | flops 15000000512 | bytes 14000000 | tf_op jit(solution)/shard_map/pallas_call | solution.py:448
  144.5 2.4 %shard_map.103 = (bf16[128,4096]{1,0:T(8,128)(2,1)}, bf16[512,384]{1,0:T(8,128)(2,1)}, bf16[512,384]{1,0:T(8,128)(2,1)}, bf16[384,512]{1,0:T(8,128)(2,1)}) custom-call(bf16[128,4096]{1,0:T(8,128)(2,1)} %get-tuple-element.12.gt, bf16[512,384]{1,0:T(8,128)(2,1)} %get-tuple-element.13.gg, bf16[512,384]{1,0:T(8,128)(2,1)} %get-tuple-element.14.gu, ...), custom_call_target="tpu_custom_call" | custom-call | tf_op jit(solution)/shard_map/pallas_call | solution.py:487

commit v3 on v2

--- a/solution.py
+++ b/solution.py
@@ -45,11 +45,11 @@
 
 
 def kernel(
-    ids, probs, tok, cot, wg, wu, wd,
-    gt, gg, gu, gd,
-    tokb, cotb, w_gu, w_d, xs, xse, ss, sse, X, XE, S, SE,
+    ids_in, probs_in, tok, cot, wg, wu, wd,
+    gt, grads,
+    ids, probs, tokb, cotb, w_gu, w_d, xs, xse, ss, sse, X, XE, S, SE,
     pick, pick_e, pick_t, pick_et, scales, pre, gh, ggu, at,
-    RG, RGE, RV, RVE, PS, PSE, RT, RTE, ring, begin, psum, gds, outs,
+    RG, RGE, RV, RVE, PS, PSE, RT, RTE, ring, begin, psum, gds,
     loc, snd, rcv, sib_s, sib_r, ring_s, ring_r,
 ):
     z = lax.axis_index("dp")
@@ -69,12 +69,16 @@
     for chip in chip_of:
         pl.semaphore_signal(barrier, inc=1, device_id=(z, chip * 2 + k), device_id_type=MESH)
     pl.semaphore_signal(barrier, inc=1, device_id=sibling, device_id_type=MESH)
+    pltpu.make_async_copy(ids_in, ids, loc.at[6]).start()
+    pltpu.make_async_copy(probs_in, probs, loc.at[7]).start()
     for j in range(J):
         pltpu.make_async_copy(tok.at[:, pl.ds(j * DS, DS)], tokb.at[j], loc.at[0]).start()
 
     def wait_bytes(ref, sem):
         pltpu.make_async_copy(ref, ref, sem).wait()
 
+    wait_bytes(ids, loc.at[6])
+    wait_bytes(probs, loc.at[7])
     id0, id1 = ids[0:1, :], ids[1:2, :]
     p0, p1 = probs[0:1, :], probs[1:2, :]
     row = iota((HALF, TOK), 0)
@@ -205,10 +209,6 @@
         fwd.wait_recv()
         pre[...] += mm(X[j], w_gu[j])
 
-    @pl.loop(J - LAG, J)
-    def _(i):
-        send_cot(i)
-
     def store_t(first, value):
         at[pl.ds(first, F), :] = mm_nt(eye(F), value).astype(BF16)
 
@@ -277,16 +277,13 @@
             end(m)
             end(n // 2 + m)
 
-    wait_bytes(SE.at[pl.ds(0, HALF), :], rcv.at[SE_AT])
-    fwd_se = to_sibling(SE.at[mine, :], SE.at[mine, :], SE_AT)
-    fwd_se.start()
-    fwd_se.wait_recv()
-    wait_bytes(w_d, loc.at[3])
-
     def forward(i):
         o = order(i)
         wait_bytes(S.at[o, pl.ds(0, HALF), :], rcv.at[S_AT + i])
         to_sibling(S.at[o, mine, :], S.at[o, mine, :], S_AT + i).start()
+
+    def fill_tail(i):
+        o = order(i)
         S[o, tail, :] = mm(unpack(o), SE[...]).astype(BF16)
 
     def here(i):
@@ -302,15 +299,28 @@
         hops(down, t, 0, (up,))
         hops(down, t, 1, (up,))
 
+    wait_bytes(SE.at[pl.ds(0, HALF), :], rcv.at[SE_AT])
+    fwd_se = to_sibling(SE.at[mine, :], SE.at[mine, :], SE_AT)
+    fwd_se.start()
     forward(0)
+    fwd_se.wait_recv()
+    fill_tail(0)
     here(0)
     begin_chains(down, S)
+
+    @pl.loop(J - LAG, J)
+    def _(i):
+        send_cot(i)
+
+    wait_bytes(w_d, loc.at[3])
     for i in range(1, 7):
         forward(i)
+        fill_tail(i)
         grad_hidden(i - 1)
         here(i)
         if i == 6:
             forward(7)
+            fill_tail(7)
         down_step((i + 1) // 2, i % 2)
     grad_hidden(6)
     here(7)
@@ -382,14 +392,13 @@
             several(2, 4, pair_grad)
             row_grad_extras()
     end_chains(down, S)
-    pltpu.make_async_copy(gds.at[pl.ds(2 * F, F), :], gd, loc.at[5]).start()
+    def out(first, rows):
+        rows = pl.ds(first, rows)
+        pltpu.make_async_copy(gds.at[rows, :], grads.at[rows, :], loc.at[5]).start()
+
+    out(2 * F, F)
     wait_bytes(RTE, rcv.at[RE_AT])
     several(0, 4, token_grad)
-    end_chains(gate_up, X)
-    out_d = pltpu.make_async_copy(gds.at[pl.ds(2 * F, F), :], gd, loc.at[5])
-    for n, dst in enumerate((gg, gu)):
-        outs[n] = mm_nt(eye(DS), gds[n * F:(n + 1) * F, :]).astype(BF16)
-        pltpu.make_async_copy(outs.at[n], dst, loc.at[6 + n]).start()
 
     def sent(ref, sem):
         wait_bytes(ref, sem)
@@ -409,53 +418,69 @@
     for at_sem in (XE_AT, SE_AT, RGE_AT):
         sent(xse, sib_s.at[at_sem])
 
-    @pl.loop(0, 24)
-    def _(v):
-        for t in range(1, 4):
-            sent(ring.at[v, t], ring_s.at[v, t])
-
     for u0, n, _ in (down, gate_up):
         for m in range(n // 2):
             sent(begin.at[0], ring_s.at[u0 + m, 0])
             sent(begin.at[0], ring_s.at[12 + u0 + n // 2 + m, 0])
 
+    @pl.loop(0, 24)
+    def _(v):
+        for t in range(1, 3):
+            sent(ring.at[v, t], ring_s.at[v, t])
+
     wait_bytes(tokb, loc.at[4])
-    out_d.wait()
-    for n, dst in enumerate((gg, gu)):
-        pltpu.make_async_copy(outs.at[n], dst, loc.at[6 + n]).wait()
-
-
-def write_out(gt, gg, gu, gd, gt_out, gg_out, gu_out, gd_out, gt_v, gg_v, gu_v, gd_v, sem):
-    whole = ((gg, gg_v, gg_out), (gu, gu_v, gu_out), (gd, gd_v, gd_out))
-    parts = [tuple(ref.at[pl.ds(32 * n, 32), :] for ref in (gt, gt_v, gt_out)) for n in range(4)]
-    parts += whole
-    reads = [pltpu.make_async_copy(src, mid, sem.at[0, n]) for n, (src, mid, _) in enumerate(parts)]
-    writes = [pltpu.make_async_copy(mid, dst, sem.at[1, n]) for n, (_, mid, dst) in enumerate(parts)]
-    for read in reads:
+    end_chains(gate_up, X)
+    out(0, 2 * F)
+
+    @pl.loop(0, 24)
+    def _(v):
+        sent(ring.at[v, 3], ring_s.at[v, 3])
+
+    wait_bytes(gds, loc.at[5])
+
+
+def write_out(gt, grads, gt_out, gg_out, gu_out, gd_out, gt_v, grads_v, turned, sem):
+    parts = [
+        pltpu.make_async_copy(grads.at[pl.ds(n * F, F), :], grads_v.at[pl.ds(n * F, F), :], sem.at[n])
+        for n in range(3)
+    ]
+    rows = [pl.ds(32 * n, 32) for n in range(4)]
+    tokens = [pltpu.make_async_copy(gt.at[r, :], gt_v.at[r, :], sem.at[3 + n]) for n, r in enumerate(rows)]
+    for read in parts + tokens:
         read.start()
-    for read, write in zip(reads, writes):
-        read.wait()
-        write.start()
-    for write in writes:
-        write.wait()
+    writes = []
+
+    def write(src, dst):
+        writes.append(pltpu.make_async_copy(src, dst, sem.at[7 + len(writes)]))
+        writes[-1].start()
+
+    for n, dst in enumerate((gg_out, gu_out)):
+        parts[n].wait()
+        turned[n] = mm_nt(eye(DS), grads_v[n * F:(n + 1) * F, :]).astype(BF16)
+        write(turned.at[n], dst)
+    parts[2].wait()
+    write(grads_v.at[pl.ds(2 * F, F), :], gd_out)
+    for n, r in enumerate(rows):
+        tokens[n].wait()
+        write(gt_v.at[r, :], gt_out.at[r, :])
+    for copy in writes:
+        copy.wait()
 
 
 def shards(tokens, cotangent, expert_ids, probs, w_gate, w_up, w_down):
     any_ = pl.BlockSpec(memory_space=pl.ANY)
-    vmem = pl.BlockSpec(memory_space=pltpu.VMEM)
     dma = pltpu.SemaphoreType.DMA
     v = pltpu.VMEM
-    gt, gg, gu, gd = pl.pallas_call(
+    gt, grads = pl.pallas_call(
         kernel,
         out_shape=(
             jax.ShapeDtypeStruct((TOK, D), BF16),
-            jax.ShapeDtypeStruct((DS, F), BF16),
-            jax.ShapeDtypeStruct((DS, F), BF16),
-            jax.ShapeDtypeStruct((F, DS), BF16),
+            jax.ShapeDtypeStruct((3 * F, DS), BF16),
         ),
-        in_specs=[vmem, vmem] + [any_] * 5,
-        out_specs=(any_,) * 4,
+        in_specs=[any_] * 7,
+        out_specs=(any_,) * 2,
         scratch_shapes=[
+            v((2, TOK), jnp.int32), v((2, TOK), F32),
             v((J, TOK, DS), BF16), v((J, TOK, DS), BF16),
             v((J, DS, 2 * F), BF16), v((J, F, DS), BF16),
             v((J, HALF, DS), BF16), v((HALF, DS), BF16),
@@ -472,7 +497,7 @@
             v((J, HALF, DS), BF16), v((HALF, DS), BF16),
             v((J, HALF, DS), BF16), v((HALF, DS), BF16),
             v((24, 4, UNIT, DS), BF16), v((12, UNIT, DS), BF16), v((16, UNIT, DS), F32),
-            v((3 * F, DS), BF16), v((2, DS, F), BF16),
+            v((3 * F, DS), BF16),
             dma((8,)), dma((23,)), dma((23,)), dma((27,)), dma((27,)),
             dma((24, 4)), dma((24, 4)),
         ],
@@ -483,14 +508,18 @@
             flops=15_000_000_000, bytes_accessed=14_000_000, transcendentals=500_000
         ),
     )(expert_ids.T, probs.T, tokens, cotangent, w_gate[0], w_up[0], w_down[0])
-    found = (gt, gg, gu, gd)
     gt, gg, gu, gd = pl.pallas_call(
         write_out,
-        out_shape=tuple(jax.ShapeDtypeStruct(a.shape, a.dtype) for a in found),
-        in_specs=[any_] * 4,
+        out_shape=(
+            jax.ShapeDtypeStruct((TOK, D), BF16),
+            jax.ShapeDtypeStruct((DS, F), BF16),
+            jax.ShapeDtypeStruct((DS, F), BF16),
+            jax.ShapeDtypeStruct((F, DS), BF16),
+        ),
+        in_specs=[any_] * 2,
         out_specs=(any_,) * 4,
-        scratch_shapes=[v(a.shape, a.dtype) for a in found] + [dma((2, 7))],
-    )(*found)
+        scratch_shapes=[v((TOK, D), BF16), v((3 * F, DS), BF16), v((2, DS, F), BF16), dma((14,))],
+    )(gt, grads)
     return gt, gg[None], gu[None], gd[None]
 
 

time: 147 us -> 147 us (level)
  no operation moved by 1% of the time
where the time goes in v3:
time: 147 us
  Pallas kernels  146 us (99%)
    pallas_call x1, Pallas kernels, shards(): pl.pallas_call(kernel, out_shape=(jax.ShapeDtypeStruct((TOK, D), BF16), j...  143 us
    pallas_call x1, Pallas kernels, shards(): pl.pallas_call(write_out, out_shape=(jax.ShapeDtypeStruct((TOK, D), BF16)...  3.27 us

profile of v3, /device:TPU:1, one launch (start us, length us, event | category | flops | bytes accessed | tf_op | source)
XLA Modules:
  0.0 146.5 jit_solution(3111593299059867649)
XLA Ops:
  0.6 142.6 %shard_map.102 = (bf16[128,4096]{1,0:T(8,128)(2,1)}, bf16[1152,512]{1,0:T(8,128)(2,1)}) custom-call(s32[2,128]{1,0:T(2,128)} %bitcast.14, f32[2,128]{1,0:T(2,128)} %bitcast.15, bf16[128,4096]{1,0:T(8,128)(2,1)} %tok.1, bf16[128,4096]{1,0:T(8,128)(2,1)} %cot.1, bf16[4096,384]{1,0:T(8,128)(2,1)} %bitcast.8, bf16[4096,384]{1,0:T(8,128)(2,1)} %bitcast.9, ...), custom_call_target="tpu_custom_call" | custom-call | flops 15000000512 | bytes 14000000 | tf_op jit(solution)/shard_map/pallas_call | solution.py:474
  143.3 3.3 %shard_map.103 = (bf16[128,4096]{1,0:T(8,128)(2,1)}, bf16[512,384]{1,0:T(8,128)(2,1)}, bf16[512,384]{1,0:T(8,128)(2,1)}, bf16[384,512]{1,0:T(8,128)(2,1)}) custom-call(bf16[128,4096]{1,0:T(8,128)(2,1)} %get-tuple-element.10.gt, bf16[1152,512]{1,0:T(8,128)(2,1)} %get-tuple-element.11.grads), custom_call_target="tpu_custom_call" | custom-call | tf_op jit(solution)/shard_map/pallas_call | solution.py:511

commit v4 on v3

--- a/solution.py
+++ b/solution.py
@@ -215,6 +215,11 @@
     gate, up = pre[:, 0:F], pre[:, F:2 * F]
     store_t(2 * F, (gate * jax.nn.sigmoid(gate) * up).astype(BF16))
 
+    def several(first, last, what):
+        @pl.loop(first, last)
+        def _(n):
+            what(n)
+
     def pass_on(v, t, src, up):
         pltpu.make_async_remote_copy(
             src_ref=src, dst_ref=ring.at[v, t],
@@ -222,21 +227,24 @@
             device_id=z_next if up else z_prev, device_id_type=MESH,
         ).start()
 
-    down, gate_up = (0, 4, 2 * F), (4, 8, 0)
+    down, gate_up = (0, 4, 2 * F, 3), (4, 8, 0, 3)
 
     def begin_chains(group, source):
-        u0, n, first = group
+        u0, n, first, lo = group
         terms = mm(at[pl.ds(first, n * UNIT), :], source[place(0, False)])
         for m in range(n):
             begin[u0 + m] = terms[m * UNIT:(m + 1) * UNIT].astype(BF16)
 
-        @pl.loop(0, n // 2)
+        @pl.loop(0, lo)
         def _(m):
             pass_on(u0 + m, 0, begin.at[u0 + m], False)
-            pass_on(12 + u0 + n // 2 + m, 0, begin.at[u0 + n // 2 + m], True)
+
+        @pl.loop(lo, n)
+        def _(m):
+            pass_on(12 + u0 + m, 0, begin.at[u0 + m], True)
 
     def terms_of(group, t, up, source):
-        u0, n, first = group
+        u0, n, first, lo = group
         terms = mm(at[pl.ds(first, n * UNIT), :], source[place(t, up)])
         for m in range(n):
             psum[up * 8 + m] = terms[m * UNIT:(m + 1) * UNIT]
@@ -252,17 +260,22 @@
         pass_on(v, t, slot_ref, up)
 
     def hops(group, t, half, ups):
-        n = group[1]
-
-        @pl.loop(0, n // 2)
-        def _(m):
-            joins = t > 1 or half == 1
+        _, n, _, lo = group
+        places = (half * n // 2, (half + 1) * n // 2)
+        if t == 1:
+            for i in range(*places):
+                for up in ups:
+                    m = i if up else (i + lo) % n
+                    hop(group, m, t, up, (m >= lo) == bool(up))
+            return
+
+        @pl.loop(*places)
+        def _(i):
             for up in ups:
-                upper = (half == 0) != bool(up)
-                hop(group, m + (n // 2 if upper else 0), t, up, joins)
+                hop(group, i if up else lax.rem(i + lo, n), t, up, True)
 
     def end_chains(group, source):
-        u0, n, first = group
+        u0, n, first, lo = group
         terms_of(group, 4, 0, source)
 
         def end(m):
@@ -272,10 +285,15 @@
             rows = pl.ds(pl.multiple_of(first + m * UNIT, UNIT), UNIT)
             gds[rows, :] = (psum[m] + came).astype(BF16)
 
-        @pl.loop(0, n // 2)
+        if n < 2 * lo:
+            several(0, n, end)
+            return
+        several(lo, n - lo, end)
+
+        @pl.loop(0, lo)
         def _(m):
             end(m)
-            end(n // 2 + m)
+            end(n - lo + m)
 
     def forward(i):
         o = order(i)
@@ -369,11 +387,6 @@
             tokb[j] = (mm(pick_t[...], RT[j]) + mm(chosen, RTE[...])).astype(BF16)
             cols = pl.ds(pl.multiple_of(j * DS, DS), DS)
             pltpu.make_async_copy(tokb.at[j], gt.at[:, cols], loc.at[4]).start()
-
-    def several(first, last, what):
-        @pl.loop(first, last)
-        def _(n):
-            what(n)
 
     begin_chains(gate_up, X)
     several(0, 4, row_grad)
@@ -418,10 +431,9 @@
     for at_sem in (XE_AT, SE_AT, RGE_AT):
         sent(xse, sib_s.at[at_sem])
 
-    for u0, n, _ in (down, gate_up):
-        for m in range(n // 2):
-            sent(begin.at[0], ring_s.at[u0 + m, 0])
-            sent(begin.at[0], ring_s.at[12 + u0 + n // 2 + m, 0])
+    for u0, n, _, lo in (down, gate_up):
+        for m in range(n):
+            sent(begin.at[0], ring_s.at[u0 + m + (0 if m < lo else 12), 0])
 
     @pl.loop(0, 24)
     def _(v):
@@ -446,7 +458,7 @@
     ]
     rows = [pl.ds(32 * n, 32) for n in range(4)]
     tokens = [pltpu.make_async_copy(gt.at[r, :], gt_v.at[r, :], sem.at[3 + n]) for n, r in enumerate(rows)]
-    for read in parts + tokens:
+    for read in tokens + parts[::-1]:
         read.start()
     writes = []
 
@@ -454,15 +466,15 @@
         writes.append(pltpu.make_async_copy(src, dst, sem.at[7 + len(writes)]))
         writes[-1].start()
 
+    for n, r in enumerate(rows):
+        tokens[n].wait()
+        write(gt_v.at[r, :], gt_out.at[r, :])
+    parts[2].wait()
+    write(grads_v.at[pl.ds(2 * F, F), :], gd_out)
     for n, dst in enumerate((gg_out, gu_out)):
         parts[n].wait()
         turned[n] = mm_nt(eye(DS), grads_v[n * F:(n + 1) * F, :]).astype(BF16)
         write(turned.at[n], dst)
-    parts[2].wait()
-    write(grads_v.at[pl.ds(2 * F, F), :], gd_out)
-    for n, r in enumerate(rows):
-        tokens[n].wait()
-        write(gt_v.at[r, :], gt_out.at[r, :])
     for copy in writes:
         copy.wait()
 

time: 147 us -> 146 us (level)
  no operation moved by 1% of the time
where the time goes in v4:
time: 146 us
  Pallas kernels  145 us (99%)
    pallas_call x1, Pallas kernels, shards(): pl.pallas_call(kernel, out_shape=(jax.ShapeDtypeStruct((TOK, D), BF16), j...  142 us
    pallas_call x1, Pallas kernels, shards(): pl.pallas_call(write_out, out_shape=(jax.ShapeDtypeStruct((TOK, D), BF16)...  3.35 us

profile of v4, /device:TPU:1, one launch (start us, length us, event | category | flops | bytes accessed | tf_op | source)
XLA Modules:
  0.0 146.1 jit_solution(14459302908399432345)
XLA Ops:
  0.6 142.1 %shard_map.102 = (bf16[128,4096]{1,0:T(8,128)(2,1)}, bf16[1152,512]{1,0:T(8,128)(2,1)}) custom-call(s32[2,128]{1,0:T(2,128)} %bitcast.14, f32[2,128]{1,0:T(2,128)} %bitcast.15, bf16[128,4096]{1,0:T(8,128)(2,1)} %tok.1, bf16[128,4096]{1,0:T(8,128)(2,1)} %cot.1, bf16[4096,384]{1,0:T(8,128)(2,1)} %bitcast.8, bf16[4096,384]{1,0:T(8,128)(2,1)} %bitcast.9, ...), custom_call_target="tpu_custom_call" | custom-call | flops 15000000512 | bytes 14000000 | tf_op jit(solution)/shard_map/pallas_call | solution.py:486
  142.7 3.4 %shard_map.103 = (bf16[128,4096]{1,0:T(8,128)(2,1)}, bf16[512,384]{1,0:T(8,128)(2,1)}, bf16[512,384]{1,0:T(8,128)(2,1)}, bf16[384,512]{1,0:T(8,128)(2,1)}) custom-call(bf16[128,4096]{1,0:T(8,128)(2,1)} %get-tuple-element.10.gt, bf16[1152,512]{1,0:T(8,128)(2,1)} %get-tuple-element.11.grads), custom_call_target="tpu_custom_call" | custom-call | tf_op jit(solution)/shard_map/pallas_call | solution.py:523

commit v5 on v4

--- a/solution.py
+++ b/solution.py
@@ -25,7 +25,7 @@
 )
 X_AT, XE_AT, S_AT, SE_AT, R_AT, RE_AT = 0, 8, 9, 17, 18, 22
 RG_AT, RGE_AT = 18, 26
-LAG = 2
+LAG = 3
 
 
 def mm(a, b):
@@ -326,13 +326,11 @@
     here(0)
     begin_chains(down, S)
 
-    @pl.loop(J - LAG, J)
-    def _(i):
-        send_cot(i)
-
     wait_bytes(w_d, loc.at[3])
     for i in range(1, 7):
         forward(i)
+        if i <= LAG:
+            send_cot(J - LAG + i - 1)
         fill_tail(i)
         grad_hidden(i - 1)
         here(i)

time: 146 us -> 146 us (level)
  no operation moved by 1% of the time
where the time goes in v5:
time: 146 us
  Pallas kernels  145 us (99%)
    pallas_call x1, Pallas kernels, shards(): pl.pallas_call(kernel, out_shape=(jax.ShapeDtypeStruct((TOK, D), BF16), j...  142 us
    pallas_call x1, Pallas kernels, shards(): pl.pallas_call(write_out, out_shape=(jax.ShapeDtypeStruct((TOK, D), BF16)...  3.36 us

profile of v5, /device:TPU:1, one launch (start us, length us, event | category | flops | bytes accessed | tf_op | source)
XLA Modules:
  0.0 145.9 jit_solution(1949655158574562129)
XLA Ops:
  0.6 141.9 %shard_map.102 = (bf16[128,4096]{1,0:T(8,128)(2,1)}, bf16[1152,512]{1,0:T(8,128)(2,1)}) custom-call(s32[2,128]{1,0:T(2,128)} %bitcast.14, f32[2,128]{1,0:T(2,128)} %bitcast.15, bf16[128,4096]{1,0:T(8,128)(2,1)} %tok.1, bf16[128,4096]{1,0:T(8,128)(2,1)} %cot.1, bf16[4096,384]{1,0:T(8,128)(2,1)} %bitcast.8, bf16[4096,384]{1,0:T(8,128)(2,1)} %bitcast.9, ...), custom_call_target="tpu_custom_call" | custom-call | flops 15000000512 | bytes 14000000 | tf_op jit(solution)/shard_map/pallas_call | solution.py:484
  142.5 3.4 %shard_map.103 = (bf16[128,4096]{1,0:T(8,128)(2,1)}, bf16[512,384]{1,0:T(8,128)(2,1)}, bf16[512,384]{1,0:T(8,128)(2,1)}, bf16[384,512]{1,0:T(8,128)(2,1)}) custom-call(bf16[128,4096]{1,0:T(8,128)(2,1)} %get-tuple-element.10.gt, bf16[1152,512]{1,0:T(8,128)(2,1)} %get-tuple-element.11.grads), custom_call_target="tpu_custom_call" | custom-call | tf_op jit(solution)/shard_map/pallas_call | solution.py:521
